TPU v7x, 512 devices: a whole 4x4x16 slice. The times are simulated.
512 devices in a mesh: dp: 16 (over y, z_lo), space: 32 (over x, z_hi, core).
Axes of the slice: x: 4, y: 4, z: 16 (z_hi: 4, z_lo: 4; z = z_hi * 4 + z_lo), core: 2. Of those that a mesh axis runs over, the one named last changes fastest.
Arguments:
- layer_input: bfloat16 [32, 32, 64, 4096], P('dp', None, None, 'space'), may hold values from -6 to 6
- cotangent: bfloat16 [32, 32, 64, 4096], P('dp', None, None, 'space'), may hold values from -6 to 6
- closure_step: int32 [32], P('dp'), may hold values from 0 to 31
- spectral_weight: float32 [64, 16, 2, 1024], P('space'), may hold values from -0.75 to 0.75
- point_weight: float32 [32, 32], replicated, may hold values from -1 to 1
- bias: float32 [32], replicated, may hold values from -4 to 4
Outputs:
- grad_input: bfloat16 [32, 32, 64, 4096], P('dp', None, None, 'space')
- grad_spectral: float32 [64, 16, 2, 1024], P('space')
- grad_point: float32 [32, 32], replicated
- grad_bias: float32 [32], replicated
All inputs are finite; a program needn't handle non-finite values.
Results may differ from a plain program's by a relative error of at most 0.001.
Values sent between devices are 32-bit elements; how exact they have to be, the bound alone decides.
A program may use at most 128 MiB of HBM per device.

v0:
```python
import math

import jax
import jax.numpy as jnp
from jax import lax
from jax.sharding import PartitionSpec as P

PRECISE = lax.Precision.HIGHEST


def contract(form, left, right):
    return jnp.einsum(form, left, right, precision=PRECISE)


def space_frequency(number):
    indices = jnp.arange(number, dtype=jnp.int32)
    return jnp.where(indices >= number // 2, indices - number, indices)


def wave_table(frequency, positions, period):
    product = frequency[:, None] * positions[None, :] % period
    angles = product.astype(jnp.float32) * (2.0 * math.pi / period)
    return (jnp.cos(angles), jnp.sin(angles))


def to_modes(values, tables, owned_modes):
    cos_x, sin_x, cos_t, sin_t = tables
    samples, channels, time_steps, local_cells = values.shape
    kept_modes = cos_t.shape[0]
    along_a = contract("sctx,mt->scmx", values, cos_t)
    along_b = contract("sctx,mt->scmx", values, sin_t)
    real_part = contract("scmx,jx->jscm", along_a, cos_x) - contract(
        "scmx,jx->jscm", along_b, sin_x
    )
    imag_part = -(
        contract("scmx,jx->jscm", along_a, sin_x) + contract("scmx,jx->jscm", along_b, cos_x)
    )
    owned_rows = lax.psum_scatter(
        jnp.stack([real_part, imag_part], 1).reshape(owned_modes * lax.axis_size("space"), 2, -1),
        "space",
        scatter_dimension=0,
        tiled=True,
    )
    owned_rows = owned_rows.reshape(owned_modes, 2, samples, channels, kept_modes)
    return (owned_rows[:, 0], owned_rows[:, 1])


def from_modes(real_part, imag_part, tables):
    cos_x, sin_x, cos_t, sin_t = tables
    owned_modes, samples, channels, kept_modes = real_part.shape
    packed = jnp.stack([real_part, imag_part], 1).reshape(owned_modes, 2, -1)
    shard_rows = lax.all_gather(packed, "space", axis=0, tiled=True)
    row_count = shard_rows.shape[0]
    rows_all = shard_rows.reshape(row_count, 2, samples, channels, kept_modes)
    upper_sum = contract("jscm,jx->scmx", rows_all[:, 0], cos_x) - contract(
        "jscm,jx->scmx", rows_all[:, 1], sin_x
    )
    lower_sum = contract("jscm,jx->scmx", rows_all[:, 0], sin_x) + contract(
        "jscm,jx->scmx", rows_all[:, 1], cos_x
    )
    return contract("scmx,mt->sctx", upper_sum, cos_t) - contract("scmx,mt->sctx", lower_sum, sin_t)


def body(layer_input, cotangent, closure_step, spectral_weight, point_weight, bias):
    samples, channels, time_steps, local_cells = layer_input.shape
    space_groups = lax.axis_size("space")
    total_cells = local_cells * space_groups
    owned_modes = spectral_weight.shape[0]
    all_modes = owned_modes * space_groups
    kept_modes = spectral_weight.shape[1]
    positions = lax.axis_index("space") * local_cells + jnp.arange(local_cells, dtype=jnp.int32)
    cos_x, sin_x = wave_table(space_frequency(all_modes), positions, total_cells)
    cos_t, sin_t = wave_table(
        jnp.arange(kept_modes, dtype=jnp.int32), jnp.arange(time_steps, dtype=jnp.int32), time_steps
    )
    tables = (cos_x, sin_x, cos_t, sin_t)
    in_scale = 1.0 / math.sqrt(total_cells * time_steps)
    out_scale = 1.0 / math.sqrt(all_modes * kept_modes)
    w_real = spectral_weight[:, :, 0].reshape(owned_modes, kept_modes, channels, channels)
    w_imag = spectral_weight[:, :, 1].reshape(owned_modes, kept_modes, channels, channels)
    values = layer_input.astype(jnp.float32)
    x_real, x_imag = to_modes(values, tables, owned_modes)
    x_real = x_real * in_scale
    x_imag = x_imag * in_scale
    y_real = contract("jmio,jsim->jsom", w_real, x_real) - contract(
        "jmio,jsim->jsom", w_imag, x_imag
    )
    y_imag = contract("jmio,jsim->jsom", w_real, x_imag) + contract(
        "jmio,jsim->jsom", w_imag, x_real
    )
    spectral = from_modes(y_real, y_imag, tables) * out_scale
    preact = spectral + contract("sitx,io->sotx", values, point_weight) + bias[None, :, None, None]
    live_steps = (jnp.arange(time_steps, dtype=jnp.int32)[None, :] >= closure_step[:, None]).astype(
        jnp.float32
    )
    masked = cotangent.astype(jnp.float32) * live_steps[:, None, :, None]
    unused, pullback = jax.vjp(jax.nn.gelu, preact)
    grad_pre = pullback(masked)[0]
    g_real, g_imag = to_modes(grad_pre, tables, owned_modes)
    g_real = g_real * out_scale
    g_imag = g_imag * out_scale
    h_real = contract("jmio,jsom->jsim", w_real, g_real) + contract(
        "jmio,jsom->jsim", w_imag, g_imag
    )
    h_imag = contract("jmio,jsom->jsim", w_real, g_imag) - contract(
        "jmio,jsom->jsim", w_imag, g_real
    )
    grad_field = (
        contract("sotx,io->sitx", grad_pre, point_weight)
        + from_modes(h_real, h_imag, tables) * in_scale
    )
    dw_real = contract("jsim,jsom->jmio", x_real, g_real) + contract(
        "jsim,jsom->jmio", x_imag, g_imag
    )
    dw_imag = contract("jsim,jsom->jmio", x_real, g_imag) - contract(
        "jsim,jsom->jmio", x_imag, g_real
    )
    spectral_part = jnp.stack([dw_real, dw_imag], 2).reshape(
        owned_modes, kept_modes, 2, channels * channels
    )
    point_part = contract("sitx,sotx->io", values, grad_pre)
    bias_part = jnp.sum(grad_pre, axis=(0, 2, 3))
    spectral_total = lax.psum(spectral_part, "dp")
    point_total, bias_total = lax.psum((point_part, bias_part), ("dp", "space"))
    all_samples = samples * lax.axis_size("dp")
    sample_scale = 1.0 / math.sqrt(all_samples)
    point_scale = 1.0 / math.sqrt(all_samples * time_steps * total_cells)
    return (
        grad_field.astype(jnp.bfloat16),
        spectral_total * sample_scale,
        point_total * point_scale,
        bias_total * point_scale,
    )


def solution(mesh):
    return jax.shard_map(
        body,
        mesh=mesh,
        in_specs=(
            P("dp", None, None, "space"),
            P("dp", None, None, "space"),
            P("dp"),
            P("space", None, None, None),
            P(),
            P(),
        ),
        out_specs=(P("dp", None, None, "space"), P("space", None, None, None), P(), P()),
        check_vma=False,
    )
```

profile of v0, /device:TPU:1, one launch (start us, length us, event | category | flops | bytes accessed | tf_op | source)
XLA Modules:
  0.0 1024.7 jit_solution(15320383387399814152)
XLA Ops:
  7.2 1.2 copy-done
  13.5 1.1 copy.72
  15.8 1.3 dynamic-slice
  17.8 2.6 fusion.25
  20.4 343.5 %all-reduce.9.cloned.1.call-done = f32[64,2,1024]{2,1,0:T(2,128)} async-done(((f32[64,2,1024]{2,1,0:T(2,128)}), f32[64,2,1024]{2,1,0:T(2,128)}) %all-reduce.9.cloned.1.call-update) | async-done | bytes 524304
  367.5 50.0 %all_gather.6 = f32[64,2,1024]{2,1,0:T(2,128)S(1)} all-gather(f32[2,2,1024]{2,1,0:T(2,128)S(1)} %copy.77), channel_id=1, replica_groups=mesh['dp'=16,'space'=32] {'space'}, dimensions={0}, use_global_device_ids=true | all-gather | bytes 540672 | tf_op jit(solution)/shard_map/all_gather | solution.py:52
  420.2 1.9 fusion.115
  422.9 4.7 fusion.227
  427.6 1.1 convolution_bitcast_fusion.1
  434.9 2.4 copy.89
  437.3 2.8 fusion.21
  440.1 103.1 %all-reduce.2 = (f32[32,32]{0,1:T(8,128)S(1)}, f32[32]{0:T(128)S(1)}) all-reduce(f32[32,32]{0,1:T(8,128)S(1)} %fusion.21, f32[32]{0:T(128)S(1)} %get-tuple-element.24), channel_id=1, replica_groups=mesh['dp'=16,'space'=32] {'dp','space'}, use_global_device_ids=true, to_apply=%region_3.4 | all-reduce | flops 1056 | bytes 8448 | tf_op jit(solution)/shard_map/psum | solution.py:124
  544.4 231.0 %all-reduce.11.cloned.1.call-done = f32[64,2,1024]{2,1,0:T(2,128)} async-done(((f32[64,2,1024]{2,1,0:T(2,128)}), f32[64,2,1024]{2,1,0:T(2,128)}) %all-reduce.11.cloned.1.call-update) | async-done | bytes 524304
  776.3 2.0 fusion.49
  778.3 2.0 fusion.56
  780.3 2.0 fusion.17
  782.5 2.0 fusion.18
  784.7 51.7 %all_gather.7 = f32[64,2,1024]{2,1,0:T(2,128)} all-gather(f32[2,2,1024]{2,1,0:T(2,128)S(1)} %copy.94), channel_id=1, replica_groups=mesh['dp'=16,'space'=32] {'space'}, dimensions={0}, use_global_device_ids=true | all-gather | bytes 540672 | tf_op jit(solution)/shard_map/all_gather | solution.py:52
  836.4 2.4 copy.95
  838.7 1.9 fusion.29
  840.6 1.8 fusion.30
  843.4 1.8 fusion.53
  846.0 3.2 fusion.107
  850.0 3.2 fusion.112
  853.2 1.8 convolution_subtract_fusion
  855.0 1.3 stack.61
  856.3 2.9 convolution_add_fusion
  859.2 1.3 stack.60
  861.5 7.9 fusion.6
  869.4 1.4 copy.102
  870.8 145.2 %all-reduce.7.cloned.1.call-done = f32[2,16,2,1024]{3,2,1,0:T(2,128)} async-done(((f32[2,16,2,1024]{3,2,1,0:T(2,128)}), f32[2,16,2,1024]{3,2,1,0:T(2,128)}) %all-reduce.7.cloned.1.call-update) | async-done | bytes 262160 | tf_op jit(solution)/shard_map/psum | solution.py:123
  1015.9 1.8 broadcast_multiply_fusion
  (86 shorter events, 25.3 us)
Async XLA Ops:
  7.2 1.2 copy-start
  7.2 356.7 %all-reduce.9.cloned.1.call-start = ((), (), s32[]{:S(2)}) async-start(), calls=%async_computation.1 | async-start | bytes 1048576
  13.4 1.3 copy-start.5
  13.5 4.3 copy-start.8
  13.5 4.3 copy-start.6
  14.6 760.7 %all-reduce.11.cloned.1.call-start = ((), (), s32[]{:S(2)}) async-start(), calls=%async_computation.2 | async-start | bytes 1048576
  15.6 349.9 %copy-start.2 = (f32[2,16,32,32]{3,2,1,0:T(8,128)}, f32[2,16,32,32]{3,2,1,0:T(8,128)S(1)}, u32[]{:S(2)}) copy-start(f32[2,16,32,32]{3,2,1,0:T(8,128)S(1)} %reshape_squeeze.6) | copy-start | bytes 393220
  15.7 351.0 %copy-start.1 = (f32[2,16,32,32]{3,2,1,0:T(8,128)}, f32[2,16,32,32]{3,2,1,0:T(8,128)S(1)}, u32[]{:S(2)}) copy-start(f32[2,16,32,32]{3,2,1,0:T(8,128)S(1)} %reshape_squeeze.7) | copy-start | bytes 393220
  420.1 2.7 copy-start.4
  420.2 2.7 copy-start.7
  420.2 2.7 copy-start.9
  437.3 578.7 %all-reduce.7.cloned.1.call-start = ((), (), s32[]{:S(2)}) async-start(), calls=%async_computation | async-start | bytes 524288 | tf_op jit(solution)/shard_map/psum | solution.py:123
  838.7 6.5 copy-start.3
Sparse Core Ops, SparseCore 0:
  14.8 349.0 all-reduce.8
  437.4 337.9 all-reduce.10
  861.6 154.3 all-reduce.6
where the time goes:
time: 1040 us; the launch traced here: 1020 us
  waiting for transfers between devices  720 us (69%)
  blocking collectives  205 us (20%)
  matrix products  62 us (6%)
  local copies, waits for them, and re-layouts  18.4 us (2%)
  between operations  15.4 us (1%)
    unnamed x5, waiting for transfers between devices  574 us
    psum x1, waiting for transfers between devices, body(): spectral_total = lax.psum(spectral_part, 'dp')  145 us
    psum x1, blocking collectives, body(): point_total, bias_total = lax.psum((point_part, bias_part), ('dp', 'space'))  103 us
    all_gather x2, blocking collectives, from_modes(): shard_rows = lax.all_gather(packed, 'space', axis=0, tiled=True)  102 us
    dot_general x39, matrix products, contract(): return jnp.einsum(form, left, right, precision=PRECISE)  62 us
  transfers between devices with their start and end apart: 3, of which 3 were waited for; matrix products, arithmetic and copies ran while one was open for 2% of the time, Pallas kernels for 0%

commit v1 on v0

v1 whole, which is shorter than its diff:
```python
import functools
import math

import jax
import jax.numpy as jnp
from jax import lax
from jax.experimental import pallas as pl
from jax.experimental.pallas import tpu as pltpu
from jax.sharding import PartitionSpec as P

F32 = jnp.float32
BF16 = jnp.bfloat16
S, C, T, X, M = 2, 32, 64, 128, 16
GROUPS = 32
NX = X * GROUPS
NN = (((1,), (0,)), ((), ()))
NT = (((1,), (1,)), ((), ()))
TWO_PI = 2.0 * math.pi
POINT_SCALE = 1.0 / math.sqrt(32 * T * NX)
SAMPLE_SCALE = 1.0 / math.sqrt(32)
IN_SCALE = 1.0 / 512.0
OUT_SCALE = 1.0 / 32.0
GELU_C = math.sqrt(2.0 / math.pi)


def iota(shape, axis):
    return lax.broadcasted_iota(jnp.int32, shape, axis)


def split(v):
    hi = v.astype(BF16)
    return hi, (v - hi.astype(F32)).astype(BF16)


def dot(a, b, dims=NN):
    return lax.dot_general(a, b, dims, preferred_element_type=F32)


def dot3(a, b, dims=NN):
    return dot(a[0], b[0], dims) + (dot(a[0], b[1], dims) + dot(a[1], b[0], dims))


def dot_exact(a, b, dims=NN):
    return lax.dot_general(a, b, dims, preferred_element_type=F32, precision=lax.Precision.HIGHEST)


def one_hot_product(rows, table):
    hi, lo = split(rows)
    n = rows.shape[0]
    both = dot(jnp.concatenate([hi, lo], axis=0), table)
    return both[:n] + both[n:]


def kernel(
    u_hbm, c_hbm, step_ref, w_hbm, pw_ref, bias_ref,
    out_hbm, dw_out, point_out, bias_out,
    u, cot, wv, pre, gp, ob,
    d1, d2, d3, d4, k1, k2, rep, rept, tile, tilet, bcol, onehot,
    ab, ul, xr, accp, accb,
    rs0, rc0, rs1, rx, rs2, rz, ag,
    dw, ry, dw1, rzl, dwf,
    small, sc_, sx, sz, sy, szl,
    local_sem, send_sem, recv_sem,
):
    dp = lax.axis_index("dp")
    sp = lax.axis_index("space")
    core = lax.rem(sp, 2)
    zh = lax.rem(sp // 2, 4)
    xx = sp // 8
    yy = dp // 4
    zl = lax.rem(dp, 4)

    def device(x=xx, z=zh, c=core, y=yy, l=zl):
        return (y * 4 + l, x * 8 + z * 2 + c)

    def peer(axis, d):
        if axis == "core":
            return device(c=1 - core)
        if axis == "x":
            return device(x=lax.rem(xx + d, 4))
        if axis == "z":
            return device(z=lax.rem(zh + d, 4))
        if axis == "y":
            return device(y=lax.rem(yy + d, 4))
        return device(l=lax.rem(zl + d, 4))

    def distances(axis):
        return (1,) if axis == "core" else (1, 2, 3)

    loads = [
        pltpu.make_async_copy(u_hbm.at[0], u.at[0], local_sem.at[0]),
        pltpu.make_async_copy(u_hbm.at[1], u.at[1], local_sem.at[1]),
        pltpu.make_async_copy(c_hbm, cot, local_sem.at[2]),
        pltpu.make_async_copy(w_hbm, wv, local_sem.at[3]),
    ]
    for load in loads:
        load.start()

    barrier = pltpu.get_barrier_semaphore()
    for axis in ("core", "x", "z", "y", "l"):
        for d in distances(axis):
            pl.semaphore_signal(barrier, inc=1, device_id=peer(axis, d), device_id_type=pl.DeviceIdType.MESH)

    row = iota((128, 256), 0)
    col = iota((128, 256), 1)
    turn = ((lax.rem(row, 16) * lax.rem(col, 64)) - 16 * (row // 64)) & 63
    base = jnp.cos(turn.astype(F32) * (TWO_PI / 64))
    hi, lo = split(jnp.where(lax.rem(row // 16, 4) == col // 64, base, 0.0))
    d1[0], d1[1] = hi, lo

    row = iota((256, 256), 0)
    col = iota((256, 256), 1)
    owner = row // 8
    j = 2 * (lax.rem(owner // 4, 4) * 8 + lax.rem(owner, 4) * 2 + owner // 16) + lax.rem(row // 2, 2)
    freq = jnp.where(j >= 32, j - 64, j)
    turn = (freq * (sp * X + lax.rem(col, 128)) + 1024 * (lax.rem(row, 2) + col // 128)) & 4095
    table = jnp.cos(turn.astype(F32) * (TWO_PI / NX))
    turned = table.T
    for q in range(2):
        hi, lo = split(jnp.where(lax.rem(row // 4, 2) == q, table, 0.0))
        d2[q, 0], d2[q, 1] = hi, lo
        hi, lo = split(jnp.where(lax.rem(col // 4, 2) == q, turned, 0.0))
        d3[q, 0], d3[q, 1] = hi, lo

    pl.semaphore_wait(barrier, 13)

    count = [0]
    sends = []

    def start(src, dst, axis, d):
        n = count[0]
        count[0] += 1
        copy = pltpu.make_async_remote_copy(
            src_ref=src, dst_ref=dst, send_sem=send_sem.at[n], recv_sem=recv_sem.at[n],
            device_id=peer(axis, d), device_id_type=pl.DeviceIdType.MESH,
        )
        copy.start()
        sends.append(copy)
        return n

    def arrived(n, dst):
        pltpu.make_async_remote_copy(
            src_ref=dst, dst_ref=dst, send_sem=send_sem.at[n], recv_sem=recv_sem.at[n],
            device_id=peer("core", 1), device_id_type=pl.DeviceIdType.MESH,
        ).wait_recv()

    def forward(s, wide, chain):
        def block(n, carry):
            if wide:
                v = gp[s, pl.ds(4 * n, 4)].reshape(256, 128)
                vh, vl = split(v)
                out = dot(d1[0], vh) + (dot(d1[1], vh) + dot(d1[0], vl))
            else:
                v = u[s, pl.ds(4 * n, 4)].reshape(256, 128)
                out = dot(d1[0], v) + dot(d1[1], v)
            hi, lo = split(out)
            ab[s, 0, n, :, 0:128] = hi[:64]
            ab[s, 0, n, :, 128:256] = hi[64:]
            ab[s, 1, n, :, 0:128] = lo[:64]
            ab[s, 1, n, :, 128:256] = lo[64:]
            return carry

        lax.fori_loop(0, 8, block, 0)
        total = None
        for q in range(2):
            right = tuple(ab[s, p, 4 * q:4 * q + 4].reshape(256, 256) for p in range(2))
            part = dot3((d2[q, 0], d2[q, 1]), right, NT)
            total = part if total is None else total + part
        rs0[chain] = total.reshape(2, 4, 4, 8, 256)

    def inverse(s, chain, finish):
        y = split(ag[chain].reshape(256, 256))
        for q in range(2):
            hi, lo = split(dot3((d3[q, 0], d3[q, 1]), y))
            for h in range(2):
                lanes = slice(128 * h, 128 * h + 128)
                for p, v in enumerate((hi, lo)):
                    ul[s, 2 * q + h, p, :, 0:128] = v[:128, lanes]
                    ul[s, 2 * q + h, p, :, 128:256] = v[128:, lanes]

        def block(n, carry):
            finish(n, dot3((d4[0], d4[1]), (ul[s, n, 0], ul[s, n, 1]), NT))
            return carry

        lax.fori_loop(0, 4, block, 0)

    mask16 = (lax.rem(iota((16, 256), 1), 16) == iota((16, 256), 0)).astype(F32)
    mask512 = (lax.rem(iota((16, 512), 1), 16) == iota((16, 512), 0)).astype(F32)

    def mix(s, own):
        spread = (own[:, None, :] * mask16[None]).reshape(128, 256)
        xr[s] = one_hot_product(spread, rep[...]).reshape(2, 2, 2, 16, 512)
        parts = []
        for b in range(2):
            re = jnp.zeros((16, 128), F32)
            im = jnp.zeros((16, 128), F32)
            for k in range(8):
                q, lanes = k // 4, slice(128 * (k % 4), 128 * (k % 4) + 128)
                whole = slice(128 * k, 128 * k + 128)
                x_re, x_im = xr[s, q, b, 0, :, lanes], xr[s, q, b, 1, :, lanes]
                w_re, w_im = wv[b, :, 0, whole], wv[b, :, 1, whole]
                re = re + (w_re * x_re - w_im * x_im)
                im = im + (w_re * x_im + w_im * x_re)
            parts += [re, im]
        wide = one_hot_product(jnp.concatenate(parts, axis=0), tilet[...])
        out = jnp.sum(wide.reshape(4, 16, 512) * mask512[None], axis=1)
        return jnp.concatenate([out[:, :256], out[:, 256:]], axis=0)

    def mix_back(s, own):
        spread = (own[:, None, :] * mask16[None]).reshape(128, 256)
        g = one_hot_product(spread[:64], tile[0]) + one_hot_product(spread[64:], tile[1])
        rows = [[None] * 8 for _ in range(2)]
        for b in range(2):
            g_re, g_im = g[32 * b:32 * b + 16], g[32 * b + 16:32 * b + 32]
            for k in range(8):
                q, lanes = k // 4, slice(128 * (k % 4), 128 * (k % 4) + 128)
                whole = slice(128 * k, 128 * k + 128)
                w_re, w_im = wv[b, :, 0, whole], wv[b, :, 1, whole]
                rows[b][k] = (w_re * g_re + w_im * g_im, w_re * g_im - w_im * g_re)
                x_re, x_im = xr[s, q, b, 0, :, lanes], xr[s, q, b, 1, :, lanes]
                at = (k // 2, slice(None), slice(128 * (k % 2), 128 * (k % 2) + 128))
                d_re = x_re * g_re + x_im * g_im
                d_im = x_re * g_im - x_im * g_re
                if s == 0:
                    dw[(2 * b,) + at] = d_re
                    dw[(2 * b + 1,) + at] = d_im
                else:
                    dw[(2 * b,) + at] += d_re
                    dw[(2 * b + 1,) + at] += d_im
        stacked = jnp.concatenate(
            [
                jnp.concatenate([rows[b][4 * q + k][p] for k in range(4)], axis=1)
                for q in range(2) for b in range(2) for p in range(2)
            ],
            axis=0,
        )
        wide = one_hot_product(stacked, rept[...])
        return jnp.sum(wide.reshape(8, 16, 256) * mask16[None], axis=1)

    def chain_of(s):
        for back in range(2):
            ch = 2 * s + back
            if back == 0:
                loads[s].wait()
                forward(s, False, ch)
            n = start(rs0.at[ch, 1 - core], rc0.at[ch], "core", 1)
            yield
            arrived(n, rc0.at[ch])
            rs1[ch] = rs0[ch, core] + rc0[ch]
            ns = [start(rs1.at[ch, lax.rem(xx + d, 4)], rx.at[ch, d - 1], "x", d) for d in (1, 2, 3)]
            yield
            for d in (1, 2, 3):
                arrived(ns[d - 1], rx.at[ch, d - 1])
            rs2[ch] = (rs1[ch, xx] + rx[ch, 0]) + (rx[ch, 1] + rx[ch, 2])
            ns = [start(rs2.at[ch, lax.rem(zh + d, 4)], rz.at[ch, d - 1], "z", d) for d in (1, 2, 3)]
            yield
            for d in (1, 2, 3):
                arrived(ns[d - 1], rz.at[ch, d - 1])
            own = (rs2[ch, zh] + rz[ch, 0]) + (rz[ch, 1] + rz[ch, 2])
            if back == 0:
                ag[ch, core, xx, zh] = mix(s, own * IN_SCALE) * OUT_SCALE
            else:
                ag[ch, core, xx, zh] = mix_back(s, own * OUT_SCALE) * IN_SCALE
            here = ag.at[ch, core, xx, zh]
            ns = [start(here, here, "z", d) for d in (1, 2, 3)]
            yield
            for d in (1, 2, 3):
                arrived(ns[d - 1], ag.at[ch, core, xx, lax.rem(zh + 4 - d, 4)])
            here = ag.at[ch, core, xx]
            ns = [start(here, here, "x", d) for d in (1, 2, 3)]
            yield
            for d in (1, 2, 3):
                arrived(ns[d - 1], ag.at[ch, core, lax.rem(xx + 4 - d, 4)])
            here = ag.at[ch, core]
            n = start(here, here, "core", 1)
            yield
            arrived(n, ag.at[ch, 1 - core])
            if back == 0:
                closure = step_ref[s]

                def finish(n, field):
                    rows = pl.ds(8 * n, 8)
                    p = field.reshape(8, 64, 128) + pre[s, rows]
                    sq = p * p
                    th = jnp.tanh(GELU_C * (p + 0.044715 * (sq * p)))
                    slope = 0.5 * (1.0 + th) + 0.5 * p * (1.0 - th * th) * (GELU_C * (1.0 + 3 * 0.044715 * sq))
                    live = (iota((8, 64, 128), 1) >= closure).astype(F32)
                    gp[s, rows] = cot[s, rows].astype(F32) * live * slope

                inverse(s, ch, finish)
                forward(s, True, ch + 1)
            else:

                def finish(n, field):
                    rows = pl.ds(8 * n, 8)
                    ob[s, rows] = (field.reshape(8, 64, 128) + pre[s, rows]).astype(BF16)

                inverse(s, ch, finish)
                pltpu.make_async_copy(ob.at[s], out_hbm.at[s], local_sem.at[4 + s]).start()

    def pointwise(s):
        def block(n, carry):
            v = u[s, :, pl.ds(16 * n, 16), :].astype(F32)
            for h in range(2):
                b = v[:, 8 * h:8 * h + 8].reshape(256, 128).astype(BF16)
                out = dot(k1[0], b) + dot(k1[1], b) + bcol[...]
                pre[s, :, pl.ds(16 * n + 8 * h, 8), :] = out.reshape(32, 8, 128)
            return carry

        lax.fori_loop(0, 4, block, 0)

    def point_back(s):
        def block(n, carry):
            v = u[s, :, pl.ds(16 * n, 16), :].astype(F32)
            for h in range(2):
                b = v[:, 8 * h:8 * h + 8].reshape(256, 128).astype(BF16)
                rows = pl.ds(16 * n + 8 * h, 8)
                g = gp[s, :, rows, :].reshape(256, 128)
                gs = split(g)
                pre[s, :, rows, :] = dot3((k2[0], k2[1]), gs).reshape(32, 8, 128)
                accp[...] += dot(b, gs[0], NT) + dot(b, gs[1], NT)
                accb[...] += g
            return carry

        lax.fori_loop(0, 4, block, 0)

    def later_tables():
        d4row = iota((64, 256), 0)
        d4col = iota((64, 256), 1)
        turn = ((lax.rem(d4col, 16) * d4row) - 16 * (d4col // 128)) & 63
        base = jnp.cos(turn.astype(F32) * (TWO_PI / 64))
        for c in range(8):
            hi, lo = split(jnp.where(lax.rem(d4col // 16, 8) == c, base, 0.0))
            d4[0, 64 * c:64 * c + 64] = hi
            d4[1, 64 * c:64 * c + 64] = lo
        rep[...] = (iota((256, 512), 0) // 16 == iota((256, 512), 1) // 32).astype(BF16)
        rept[...] = (iota((512, 256), 0) // 32 == iota((512, 256), 1) // 16).astype(BF16)
        for q in range(2):
            tile[q] = (iota((256, 128), 0) // 16 + 16 * q == lax.rem(iota((256, 128), 1), 32)).astype(BF16)
        tilet[...] = (lax.rem(iota((128, 512), 0), 32) == iota((128, 512), 1) // 16).astype(BF16)

    def point_tables():
        pick = (iota((256, 32), 0) // 8 == iota((256, 32), 1)).astype(F32)
        onehot[...] = pick
        e = pick.astype(BF16)
        same = lax.rem(iota((256, 256), 0), 8) == lax.rem(iota((256, 256), 1), 8)
        for p, v in enumerate(split(pw_ref[...])):
            k2[p] = jnp.where(same, dot(dot(e, v).astype(BF16), e, NT), 0.0).astype(BF16)
            k1[p] = jnp.where(same, dot(dot(e, v, NT).astype(BF16), e, NT), 0.0).astype(BF16)
        column = jnp.sum(pick * bias_ref[...], axis=1, keepdims=True)
        bcol[...] = jnp.broadcast_to(column, (256, 128))
        accp[...] = jnp.zeros((256, 256), F32)
        accb[...] = jnp.zeros((256, 128), F32)

    def small_sum():
        same = (lax.rem(iota((256, 256), 0), 8) == lax.rem(iota((256, 256), 1), 8)).astype(F32)
        by_row = dot_exact((iota((32, 256), 1) // 8 == iota((32, 256), 0)).astype(F32), accp[...] * same)
        four = (iota((256, 128), 0) // 8 == lax.rem(iota((256, 128), 1), 32)).astype(F32)
        grid = dot_exact(by_row, four)
        grid = jnp.where(lax.rem(iota((32, 128), 0), 4) == iota((32, 128), 1) // 32, grid, 0.0)
        small[0, 0:8] = dot_exact((iota((8, 32), 1) // 4 == iota((8, 32), 0)).astype(F32), grid)
        column = jnp.sum(accb[...], axis=1, keepdims=True)
        line = jnp.sum(column * four, axis=0, keepdims=True)
        small[0, 8:16] = jnp.broadcast_to(line, (8, 128))
        n = start(small.at[0], sc_, "core", 1)
        yield
        arrived(n, sc_)
        small[1] = small[0] + sc_[...]
        for k, (axis, got) in enumerate((("x", sx), ("z", sz), ("y", sy), ("l", szl))):
            ns = [start(small.at[1 + k], got.at[d - 1], axis, d) for d in (1, 2, 3)]
            yield
            for d in (1, 2, 3):
                arrived(ns[d - 1], got.at[d - 1])
            small[2 + k] = (small[1 + k] + got[0]) + (got[1] + got[2])
        total = small[5] * POINT_SCALE
        spread = dot_exact((iota((32, 8), 0) // 4 == iota((32, 8), 1)).astype(F32), total[0:8])
        spread = jnp.where(lax.rem(iota((32, 128), 0), 4) == iota((32, 128), 1) // 32, spread, 0.0)
        point_out[...] = dot_exact(spread, (lax.rem(iota((128, 32), 0), 32) == iota((128, 32), 1)).astype(F32))
        bias_out[...] = total[8:9, 0:32]

    def weight_sum():
        ns = [start(dw.at[lax.rem(yy + d, 4)], ry.at[d - 1], "y", d) for d in (1, 2, 3)]
        yield
        for d in (1, 2, 3):
            arrived(ns[d - 1], ry.at[d - 1])
        dw1[...] = (dw[yy] + ry[0]) + (ry[1] + ry[2])
        ns = [start(dw1.at[lax.rem(zl + d, 4)], rzl.at[d - 1], "l", d) for d in (1, 2, 3)]
        yield
        for d in (1, 2, 3):
            arrived(ns[d - 1], rzl.at[d - 1])
        dwf[yy, zl] = ((dw1[zl] + rzl[0]) + (rzl[1] + rzl[2])) * SAMPLE_SCALE
        here = dwf.at[yy, zl]
        ns = [start(here, here, "l", d) for d in (1, 2, 3)]
        yield
        for d in (1, 2, 3):
            arrived(ns[d - 1], dwf.at[yy, lax.rem(zl + 4 - d, 4)])
        here = dwf.at[yy]
        ns = [start(here, here, "y", d) for d in (1, 2, 3)]
        yield
        for d in (1, 2, 3):
            arrived(ns[d - 1], dwf.at[lax.rem(yy + 4 - d, 4)])
        pltpu.make_async_copy(dwf, dw_out, local_sem.at[6]).start()

    a, b = chain_of(0), chain_of(1)
    smalls, weights = small_sum(), weight_sum()

    def go(*parts):
        for part in parts:
            next(part, None)

    go(a, b)
    later_tables()
    point_tables()
    go(a, b)
    pointwise(0)
    go(a, b)
    loads[3].wait()
    go(a, b)
    pointwise(1)
    go(a, b)
    go(a, b)
    loads[2].wait()
    go(a, b)
    point_back(0)
    go(a, b)
    point_back(1)
    go(smalls)
    go(a, b)
    go(smalls)
    go(a, b)
    go(weights, smalls)
    go(a, b)
    go(weights, smalls)
    go(a, b)
    go(weights, smalls)
    go(a)
    go(weights, smalls)
    go(b)
    go(weights)

    for copy in sends:
        copy.wait_send()
    pltpu.make_async_copy(ob.at[0], out_hbm.at[0], local_sem.at[4]).wait()
    pltpu.make_async_copy(ob.at[1], out_hbm.at[1], local_sem.at[5]).wait()
    pltpu.make_async_copy(dwf, dw_out, local_sem.at[6]).wait()


COPIES = 4 * 14 + 13 + 12


def body(layer_input, cotangent, closure_step, spectral_weight, point_weight, bias):
    anywhere = pl.BlockSpec(memory_space=pl.ANY)
    vmem = pl.BlockSpec(memory_space=pltpu.VMEM)
    V = pltpu.VMEM
    scratch = [
        V((S, C, T, X), BF16), V((S, C, T, X), BF16), V((2, 16, 2, 1024), F32),
        V((S, C, T, X), F32), V((S, C, T, X), F32), V((S, C, T, X), BF16),
        V((2, 128, 256), BF16), V((2, 2, 256, 256), BF16), V((2, 2, 256, 256), BF16), V((2, 512, 256), BF16),
        V((2, 256, 256), BF16), V((2, 256, 256), BF16),
        V((256, 512), BF16), V((512, 256), BF16), V((2, 256, 128), BF16), V((128, 512), BF16),
        V((256, 128), F32), V((256, 32), F32),
        V((S, 2, 8, 64, 256), BF16), V((S, 4, 2, 128, 256), BF16), V((S, 2, 2, 2, 16, 512), F32),
        V((256, 256), F32), V((256, 128), F32),
        V((4, 2, 4, 4, 8, 256), F32), V((4, 4, 4, 8, 256), F32), V((4, 4, 4, 8, 256), F32),
        V((4, 3, 4, 8, 256), F32), V((4, 4, 8, 256), F32), V((4, 3, 8, 256), F32), V((4, 2, 4, 4, 8, 256), F32),
        V((4, 4, 16, 256), F32), V((3, 4, 16, 256), F32), V((4, 16, 256), F32), V((3, 16, 256), F32),
        V((4, 4, 16, 256), F32),
        V((6, 16, 128), F32), V((16, 128), F32), V((3, 16, 128), F32), V((3, 16, 128), F32),
        V((3, 16, 128), F32), V((3, 16, 128), F32),
        pltpu.SemaphoreType.DMA((7,)), pltpu.SemaphoreType.DMA((COPIES,)), pltpu.SemaphoreType.DMA((COPIES,)),
    ]
    grad, dw, point, bias_grad = pl.pallas_call(
        kernel,
        out_shape=(
            jax.ShapeDtypeStruct((S, C, T, X), BF16),
            jax.ShapeDtypeStruct((4, 4, 16, 256), F32),
            jax.ShapeDtypeStruct((C, C), F32),
            jax.ShapeDtypeStruct((1, C), F32),
        ),
        in_specs=[anywhere, anywhere, pl.BlockSpec(memory_space=pltpu.SMEM), anywhere, vmem, vmem],
        out_specs=(anywhere, anywhere, vmem, vmem),
        scratch_shapes=scratch,
        compiler_params=pltpu.CompilerParams(
            collective_id=0, has_side_effects=True, vmem_limit_bytes=48 * 1024 * 1024
        ),
    )(layer_input, cotangent, closure_step, spectral_weight, point_weight, bias.reshape(1, C))
    dw = dw.reshape(2, 2, 4, 16, 256).transpose(0, 3, 1, 2, 4).reshape(2, 16, 2, 1024)
    return grad, dw, point, bias_grad.reshape(C)


def solution(mesh):
    return jax.shard_map(
        body,
        mesh=mesh,
        in_specs=(
            P("dp", None, None, "space"),
            P("dp", None, None, "space"),
            P("dp"),
            P("space", None, None, None),
            P(),
            P(),
        ),
        out_specs=(P("dp", None, None, "space"), P("space", None, None, None), P(), P()),
        check_vma=False,
    )
```

time: 1040 us -> 103 us (0.10); the launches traced: 1020 us -> 101 us
  waiting for transfers between devices: 720 us -> 0 us
  blocking collectives: 205 us -> 0 us
  Pallas kernels: 0 us -> 92.4 us
  matrix products: 62 us -> 0 us
  between operations: 15.4 us -> 0.67 us
  local copies, waits for them, and re-layouts: 18.4 us -> 7.96 us
    unnamed x5 -> x0, waiting for transfers between devices: 574 us -> none
    psum x1 -> x0, waiting for transfers between devices: 145 us -> none  [body(): spectral_total = lax.psum(spectral_part, 'dp')]
    psum x1 -> x0, blocking collectives: 103 us -> none  [body(): point_total, bias_total = lax.psum((point_part, bias_part), ('dp', 'space'))]
    all_gather x2 -> x0, blocking collectives: 102 us -> none  [from_modes(): shard_rows = lax.all_gather(packed, 'space', axis=0, tiled=True)]
    pallas_call x0 -> x1, Pallas kernels: none -> 92.4 us  [body(): pl.pallas_call(kernel, out_shape=(jax.ShapeDtypeStruct((S, C, T, X), BF16...]
    dot_general x39 -> x0, matrix products: 62 us -> none  [contract(): return jnp.einsum(form, left, right, precision=PRECISE)]
  transfers between devices with their start and end apart: 3 -> 0, of which waited for: 3 -> 0; matrix products, arithmetic and copies ran while one was open for 2% -> 0% of each run, Pallas kernels for 0% -> 0%
where the time goes in v1:
time: 103 us; the launch traced here: 101 us
  Pallas kernels  92.4 us (90%)
  local copies, waits for them, and re-layouts  7.96 us (8%)
    pallas_call x1, Pallas kernels, body(): pl.pallas_call(kernel, out_shape=(jax.ShapeDtypeStruct((S, C, T, X), BF16...  92.4 us
    unnamed x15, local copies, waits for them, and re-layouts  6.86 us

profile of v1, /device:TPU:1, one launch (start us, length us, event | category | flops | bytes accessed | tf_op | source)
XLA Modules:
  0.0 101.0 jit_solution(14899714867882486900)
XLA Ops:
  0.6 0.0 copy-start.5
  0.6 0.0 copy-start.4
  0.7 0.6 copy-done.5
  1.3 0.0 copy-done.4
  1.3 0.0 copy-start
  1.3 1.2 %copy-done = bf16[2,32,64,128]{3,2,1,0:T(8,128)(2,1)S(1)} copy-done((bf16[2,32,64,128]{3,2,1,0:T(8,128)(2,1)S(1)}, bf16[2,32,64,128]{3,2,1,0:T(8,128)(2,1)}, u32[]{:S(2)}) %copy-start) | copy-done | bytes 1048600
  2.5 0.0 copy-start.1
  2.5 1.2 %copy-done.1 = bf16[2,32,64,128]{3,2,1,0:T(8,128)(2,1)S(1)} copy-done((bf16[2,32,64,128]{3,2,1,0:T(8,128)(2,1)S(1)}, bf16[2,32,64,128]{3,2,1,0:T(8,128)(2,1)}, u32[]{:S(2)}) %copy-start.1) | copy-done | bytes 1048600
  3.8 0.0 copy-start.2
  3.8 0.9 copy-done.2
  4.7 0.0 copy-start.3
  4.7 0.7 copy-done.3
  5.4 92.4 %shard_map.93 = (bf16[2,32,64,128]{3,2,1,0:T(8,128)(2,1)S(1)}, f32[4,4,16,256]{3,2,1,0:T(8,128)S(1)}, f32[32,32]{1,0:T(8,128)S(1)}, f32[1,32]{1,0:T(1,128)S(1)}) custom-call(bf16[2,32,64,128]{3,2,1,0:T(8,128)(2,1)S(1)} %copy-done, bf16[2,32,64,128]{3,2,1,0:T(8,128)(2,1)S(1)} %copy-done.1, s32[2]{0:T(128)S(1)} %copy-done.4, f32[2,16,2,1024]{3,2,1,0:T(2,128)S(1)} %copy-done.2, ...), custom_call_target="tpu_custom_call" | custom-call | tf_op jit(solution)/shard_map/pallas_call | solution.py:472
  97.8 0.2 copy.10
  98.0 0.9 reshape.22
  99.0 1.0 copy.14
  99.9 0.6 copy.15
  100.5 0.5 copy.16
Async XLA Ops:
  0.6 0.7 copy-start.5
  0.6 0.7 copy-start.4
  1.3 1.2 %copy-start = (bf16[2,32,64,128]{3,2,1,0:T(8,128)(2,1)S(1)}, bf16[2,32,64,128]{3,2,1,0:T(8,128)(2,1)}, u32[]{:S(2)}) copy-start(bf16[2,32,64,128]{3,2,1,0:T(8,128)(2,1)} %u_hbm.1) | copy-start | bytes 3145732
  2.5 1.2 %copy-start.1 = (bf16[2,32,64,128]{3,2,1,0:T(8,128)(2,1)S(1)}, bf16[2,32,64,128]{3,2,1,0:T(8,128)(2,1)}, u32[]{:S(2)}) copy-start(bf16[2,32,64,128]{3,2,1,0:T(8,128)(2,1)} %c_hbm.1) | copy-start | bytes 3145732
  3.8 0.9 copy-start.2
  4.7 0.7 copy-start.3

commit v2 on v1

v2 whole, which is shorter than its diff:
```python
import functools
import math

import jax
import jax.numpy as jnp
from jax import lax
from jax.experimental import pallas as pl
from jax.experimental.pallas import tpu as pltpu
from jax.sharding import PartitionSpec as P

F32 = jnp.float32
BF16 = jnp.bfloat16
S, C, T, X, M = 2, 32, 64, 128, 16
GROUPS = 32
NX = X * GROUPS
NN = (((1,), (0,)), ((), ()))
NT = (((1,), (1,)), ((), ()))
TWO_PI = 2.0 * math.pi
POINT_SCALE = 1.0 / math.sqrt(32 * T * NX)
SAMPLE_SCALE = 1.0 / math.sqrt(32)
IN_SCALE = 1.0 / 512.0
OUT_SCALE = 1.0 / 32.0
GELU_C = math.sqrt(2.0 / math.pi)


def iota(shape, axis):
    return lax.broadcasted_iota(jnp.int32, shape, axis)


def wave(turn):
    near = turn + 512
    t = ((near & 1023) - 512).astype(F32) * (TWO_PI / NX)
    quarter = (near >> 10) & 3
    sq = t * t
    even = 1.0 + sq * (-1 / 2 + sq * (1 / 24 + sq * (-1 / 720 + sq * (1 / 40320))))
    odd = t * (1.0 + sq * (-1 / 6 + sq * (1 / 120 + sq * (-1 / 5040 + sq * (1 / 362880)))))
    value = jnp.where((quarter & 1) == 0, even, odd)
    return jnp.where(((quarter + 1) & 2) == 0, value, -value)


def split(v):
    hi = v.astype(BF16)
    return hi, (v - hi.astype(F32)).astype(BF16)


def dot(a, b, dims=NN):
    return lax.dot_general(a, b, dims, preferred_element_type=F32)


def dot3(a, b, dims=NN):
    return dot(a[0], b[0], dims) + (dot(a[0], b[1], dims) + dot(a[1], b[0], dims))


def dot_exact(a, b, dims=NN):
    return lax.dot_general(a, b, dims, preferred_element_type=F32, precision=lax.Precision.HIGHEST)


def one_hot_product(rows, table):
    hi, lo = split(rows)
    n = rows.shape[0]
    both = dot(jnp.concatenate([hi, lo], axis=0), table)
    return both[:n] + both[n:]


def kernel(
    u_hbm, c_hbm, step_ref, w_hbm, pw_ref, bias_ref,
    out_hbm, dw_out, point_out, bias_out,
    u, cot, wv, pw, bv, pre, gp, ob,
    d1, d2, d3, d4, k1, k2, rep, rept, tile, tilet, bcol, onehot,
    ab, ul, xr, accp, accb,
    rs0, rcx, rs1, rz, mine, ag,
    dw, ry, dw1, rzl, dwf,
    small, scx, sz, sy, szl,
    local_sem, send_sem, recv_sem,
):
    dp = lax.axis_index("dp")
    sp = lax.axis_index("space")
    core = lax.rem(sp, 2)
    zh = lax.rem(sp // 2, 4)
    xx = sp // 8
    yy = dp // 4
    zl = lax.rem(dp, 4)

    def device(x=xx, z=zh, c=core, y=yy, l=zl):
        return (y * 4 + l, x * 8 + z * 2 + c)

    zl2 = lax.rem(zl + 2, 4)
    first = jnp.where(zl < 2, 1, 2)
    others = [(0, 1), (0, 2), (0, 3), (1, 0), (1, 1), (1, 2), (1, 3)]

    def plane(dc, d):
        return device(x=lax.rem(xx + d, 4), c=lax.rem(core + dc, 2))

    def owner_of(i):
        return device(z=lax.rem(zh + first + i, 4), l=zl2)

    def served(i):
        return device(z=lax.rem(zh + first + 5 - i, 4), l=zl2)

    def peer(axis, d):
        if axis == "y":
            return device(y=lax.rem(yy + d, 4))
        return device(l=lax.rem(zl + d, 4))

    loads = [
        pltpu.make_async_copy(u_hbm.at[0], u.at[0], local_sem.at[0]),
        pltpu.make_async_copy(u_hbm.at[1], u.at[1], local_sem.at[1]),
        pltpu.make_async_copy(c_hbm, cot, local_sem.at[2]),
        pltpu.make_async_copy(w_hbm, wv, local_sem.at[3]),
        pltpu.make_async_copy(pw_ref, pw, local_sem.at[7]),
        pltpu.make_async_copy(bias_ref, bv, local_sem.at[8]),
    ]
    for load in loads:
        load.start()

    barrier = pltpu.get_barrier_semaphore()
    greeted = [plane(*o) for o in others] + [owner_of(i) for i in range(4)]
    greeted += [peer(axis, d) for axis in ("y", "l") for d in (1, 2, 3)]
    for who in greeted:
        pl.semaphore_signal(barrier, inc=1, device_id=who, device_id_type=pl.DeviceIdType.MESH)

    row = iota((128, 256), 0)
    col = iota((128, 256), 1)
    base = wave((((row & 15) * (col & 63)) - 16 * (row >> 6)) * 64)
    hi, lo = split(jnp.where(((row >> 4) & 3) == (col >> 6), base, 0.0))
    d1[0:128], d1[128:256] = hi, lo

    row = iota((256, 256), 0)
    col = iota((256, 256), 1)
    owner = row >> 3
    owner_z = (zh + first + 2 * (owner >> 4) + (owner & 1)) & 3
    j = 2 * (((owner >> 1) & 3) * 8 + owner_z * 2 + ((owner >> 3) & 1)) + ((row >> 1) & 1)
    freq = jnp.where(j >= 32, j - 64, j)
    table = wave(freq * (sp * X + (col & 127)) + 1024 * ((row & 1) + (col >> 7)))
    turned = table.T
    for q in range(2):
        hi, lo = split(jnp.where(((row >> 2) & 1) == q, table, 0.0))
        d2[q, 0], d2[q, 1] = hi, lo
        hi, lo = split(jnp.where(((col >> 2) & 1) == q, turned, 0.0))
        d3[q, 0], d3[q, 1] = hi, lo

    count = [0]
    sends = []

    def start(src, dst, who):
        n = count[0]
        count[0] += 1
        copy = pltpu.make_async_remote_copy(
            src_ref=src, dst_ref=dst, send_sem=send_sem.at[n], recv_sem=recv_sem.at[n],
            device_id=who, device_id_type=pl.DeviceIdType.MESH,
        )
        copy.start()
        sends.append(copy)
        return n

    def arrived(n, dst):
        pltpu.make_async_remote_copy(
            src_ref=dst, dst_ref=dst, send_sem=send_sem.at[n], recv_sem=recv_sem.at[n],
            device_id=plane(1, 0), device_id_type=pl.DeviceIdType.MESH,
        ).wait_recv()

    def forward(s, wide, chain):
        def block(n, carry):
            if wide:
                v = jnp.concatenate(split(gp[s, pl.ds(4 * n, 4)].reshape(256, 128)), axis=1)
                both = dot(d1[...], v)
                out = both[:128, :128] + (both[128:, :128] + both[:128, 128:])
            else:
                both = dot(d1[...], u[s, pl.ds(4 * n, 4)].reshape(256, 128))
                out = both[:128] + both[128:]
            hi, lo = split(out)
            ab[s, 0, n, :, 0:128] = hi[:64]
            ab[s, 0, n, :, 128:256] = hi[64:]
            ab[s, 1, n, :, 0:128] = lo[:64]
            ab[s, 1, n, :, 128:256] = lo[64:]
            return carry

        lax.fori_loop(0, 8, block, 0)
        total = None
        for q in range(2):
            right = tuple(ab[s, p, 4 * q:4 * q + 4].reshape(256, 256) for p in range(2))
            part = dot3((d2[q, 0], d2[q, 1]), right, NT)
            total = part if total is None else total + part
        rs0[chain] = total.reshape(2, 2, 4, 2, 8, 256)

    def inverse(s, chain, finish):
        y = split(ag[chain].reshape(256, 256))
        for q in range(2):
            hi, lo = split(dot3((d3[q, 0], d3[q, 1]), y))
            for h in range(2):
                lanes = slice(128 * h, 128 * h + 128)
                for p, v in enumerate((hi, lo)):
                    ul[s, 2 * q + h, 128 * p:128 * p + 128, 0:128] = v[:128, lanes]
                    ul[s, 2 * q + h, 128 * p:128 * p + 128, 128:256] = v[128:, lanes]

        def block(n, carry):
            both = dot(d4[0], ul[s, n], NT)
            finish(n, both[:, :128] + (both[:, 128:] + dot(d4[1], ul[s, n, 0:128], NT)))
            return carry

        lax.fori_loop(0, 4, block, 0)

    mask16 = ((iota((16, 256), 1) & 15) == iota((16, 256), 0)).astype(F32)
    mask512 = ((iota((16, 512), 1) & 15) == iota((16, 512), 0)).astype(F32)

    def mix(s, own):
        spread = (own[:, None, :] * mask16[None]).reshape(128, 256)
        xr[s] = one_hot_product(spread, rep[...]).reshape(2, 2, 2, 16, 512)
        parts = []
        for b in range(2):
            re = jnp.zeros((16, 128), F32)
            im = jnp.zeros((16, 128), F32)
            for k in range(8):
                q, lanes = k // 4, slice(128 * (k % 4), 128 * (k % 4) + 128)
                whole = slice(128 * k, 128 * k + 128)
                x_re, x_im = xr[s, q, b, 0, :, lanes], xr[s, q, b, 1, :, lanes]
                w_re, w_im = wv[b, :, 0, whole], wv[b, :, 1, whole]
                re = re + (w_re * x_re - w_im * x_im)
                im = im + (w_re * x_im + w_im * x_re)
            parts += [re, im]
        wide = one_hot_product(jnp.concatenate(parts, axis=0), tilet[...])
        out = jnp.sum(wide.reshape(4, 16, 512) * mask512[None], axis=1)
        return jnp.concatenate([out[:, :256], out[:, 256:]], axis=0)

    def mix_back(s, own, after):
        spread = (own[:, None, :] * mask16[None]).reshape(128, 256)
        g = one_hot_product(spread[:64], tile[0]) + one_hot_product(spread[64:], tile[1])
        gs = [(g[32 * b:32 * b + 16], g[32 * b + 16:32 * b + 32]) for b in range(2)]
        for b in range(2):
            g_re, g_im = gs[b]
            for k in range(8):
                q, lanes = k // 4, slice(128 * (k % 4), 128 * (k % 4) + 128)
                x_re, x_im = xr[s, q, b, 0, :, lanes], xr[s, q, b, 1, :, lanes]
                at = (k // 2, slice(None), slice(128 * (k % 2), 128 * (k % 2) + 128))
                d_re = x_re * g_re + x_im * g_im
                d_im = x_re * g_im - x_im * g_re
                if s == 0:
                    dw[(2 * b,) + at] = d_re
                    dw[(2 * b + 1,) + at] = d_im
                else:
                    dw[(2 * b,) + at] += d_re
                    dw[(2 * b + 1,) + at] += d_im
        after()
        rows = [[None] * 8 for _ in range(2)]
        for b in range(2):
            g_re, g_im = gs[b]
            for k in range(8):
                whole = slice(128 * k, 128 * k + 128)
                w_re, w_im = wv[b, :, 0, whole], wv[b, :, 1, whole]
                rows[b][k] = (w_re * g_re + w_im * g_im, w_re * g_im - w_im * g_re)
        stacked = jnp.concatenate(
            [
                jnp.concatenate([rows[b][4 * q + k][p] for k in range(4)], axis=1)
                for q in range(2) for b in range(2) for p in range(2)
            ],
            axis=0,
        )
        wide = one_hot_product(stacked, rept[...])
        return jnp.sum(wide.reshape(8, 16, 256) * mask16[None], axis=1)

    def chain_of(s):
        for back in range(2):
            ch = 2 * s + back
            if back == 0:
                loads[s].wait()
                forward(s, False, ch)
                yield
            ns = [
                [start(rs0.at[ch, far, lax.rem(core + dc, 2), lax.rem(xx + d, 4)], rcx.at[ch, far, p], plane(dc, d))
                 for p, (dc, d) in enumerate(others)]
                for far in range(2)
            ]
            yield
            zs = []
            for far in range(2):
                total = rs0[ch, far, core, xx]
                for p in range(7):
                    arrived(ns[far][p], rcx.at[ch, far, p])
                    total = total + rcx[ch, far, p]
                rs1[ch, far] = total
                zs += [start(rs1.at[ch, far, k], rz.at[ch, 2 * far + k], owner_of(2 * far + k)) for k in range(2)]
                yield
            for i in (2, 3, 0, 1):
                arrived(zs[i], rz.at[ch, i])
            own = (rz[ch, 0] + rz[ch, 1]) + (rz[ch, 2] + rz[ch, 3])
            if back == 0:
                mine[ch] = mix(s, own * IN_SCALE) * OUT_SCALE
            else:
                mine[ch] = mix_back(s, own * OUT_SCALE, lambda: next(weights) if s == 1 else None) * IN_SCALE
            zs = [start(mine.at[ch], ag.at[ch, i // 2, core, xx, i % 2], served(i)) for i in range(4)]
            yield
            ns = [None, None]
            for far in (1, 0):
                for k in range(2):
                    arrived(zs[2 * far + k], ag.at[ch, far, core, xx, k])
                here = ag.at[ch, far, core, xx]
                ns[far] = [start(here, here, plane(dc, d)) for dc, d in others]
                yield
            for far in (1, 0):
                for p, (dc, d) in enumerate(others):
                    arrived(ns[far][p], ag.at[ch, far, lax.rem(core + dc, 2), lax.rem(xx + 4 - d, 4)])
            if back == 0:
                closure = step_ref[s]

                def finish(n, field):
                    rows = pl.ds(8 * n, 8)
                    p = field.reshape(8, 64, 128) + pre[s, rows]
                    sq = p * p
                    th = jnp.tanh(GELU_C * (p + 0.044715 * (sq * p)))
                    slope = 0.5 * (1.0 + th) + 0.5 * p * (1.0 - th * th) * (GELU_C * (1.0 + 3 * 0.044715 * sq))
                    live = (iota((8, 64, 128), 1) >= closure).astype(F32)
                    gp[s, rows] = cot[s, rows].astype(F32) * live * slope

                inverse(s, ch, finish)
                forward(s, True, ch + 1)
            else:

                def finish(n, field):
                    rows = pl.ds(8 * n, 8)
                    ob[s, rows] = (field.reshape(8, 64, 128) + pre[s, rows]).astype(BF16)

                inverse(s, ch, finish)
                pltpu.make_async_copy(ob.at[s], out_hbm.at[s], local_sem.at[4 + s]).start()

    def pointwise(s):
        def block(n, carry):
            v = u[s, :, pl.ds(16 * n, 16), :].astype(F32)
            for h in range(2):
                b = v[:, 8 * h:8 * h + 8].reshape(256, 128).astype(BF16)
                out = dot(k1[0], b) + dot(k1[1], b) + bcol[...]
                pre[s, :, pl.ds(16 * n + 8 * h, 8), :] = out.reshape(32, 8, 128)
            return carry

        lax.fori_loop(0, 4, block, 0)

    def point_back(s):
        def block(n, carry):
            v = u[s, :, pl.ds(16 * n, 16), :].astype(F32)
            for h in range(2):
                b = v[:, 8 * h:8 * h + 8].reshape(256, 128).astype(BF16)
                rows = pl.ds(16 * n + 8 * h, 8)
                g = gp[s, :, rows, :].reshape(256, 128)
                gs = split(g)
                pre[s, :, rows, :] = dot3((k2[0], k2[1]), gs).reshape(32, 8, 128)
                accp[...] += dot(b, gs[0], NT) + dot(b, gs[1], NT)
                accb[...] += g
            return carry

        lax.fori_loop(0, 4, block, 0)

    def later_tables():
        d4row = iota((64, 256), 0)
        d4col = iota((64, 256), 1)
        base = wave((((d4col & 15) * d4row) - 16 * (d4col >> 7)) * 64)
        for c in range(8):
            hi, lo = split(jnp.where(((d4col >> 4) & 7) == c, base, 0.0))
            d4[0, 64 * c:64 * c + 64] = hi
            d4[1, 64 * c:64 * c + 64] = lo
        rep[...] = ((iota((256, 512), 0) >> 4) == (iota((256, 512), 1) >> 5)).astype(BF16)
        rept[...] = ((iota((512, 256), 0) >> 5) == (iota((512, 256), 1) >> 4)).astype(BF16)
        for q in range(2):
            tile[q] = ((iota((256, 128), 0) >> 4) + 16 * q == (iota((256, 128), 1) & 31)).astype(BF16)
        tilet[...] = ((iota((128, 512), 0) & 31) == (iota((128, 512), 1) >> 4)).astype(BF16)

    def point_tables():
        pick = ((iota((256, 32), 0) >> 3) == iota((256, 32), 1)).astype(F32)
        onehot[...] = pick
        e = pick.astype(BF16)
        same = (iota((256, 256), 0) & 7) == (iota((256, 256), 1) & 7)
        for p, v in enumerate(split(pw[...])):
            k2[p] = jnp.where(same, dot(dot(e, v).astype(BF16), e, NT), 0.0).astype(BF16)
            k1[p] = jnp.where(same, dot(dot(e, v, NT).astype(BF16), e, NT), 0.0).astype(BF16)
        column = jnp.sum(pick * bv[...], axis=1, keepdims=True)
        bcol[...] = jnp.broadcast_to(column, (256, 128))
        accp[...] = jnp.zeros((256, 256), F32)
        accb[...] = jnp.zeros((256, 128), F32)

    def small_sum():
        same = ((iota((256, 256), 0) & 7) == (iota((256, 256), 1) & 7)).astype(F32)
        by_row = dot_exact(((iota((32, 256), 1) >> 3) == iota((32, 256), 0)).astype(F32), accp[...] * same)
        four = ((iota((256, 128), 0) >> 3) == (iota((256, 128), 1) & 31)).astype(F32)
        grid = dot_exact(by_row, four)
        grid = jnp.where((iota((32, 128), 0) & 3) == (iota((32, 128), 1) >> 5), grid, 0.0)
        small[0, 0:8] = dot_exact(((iota((8, 32), 1) >> 2) == iota((8, 32), 0)).astype(F32), grid)
        column = jnp.sum(accb[...], axis=1, keepdims=True)
        line = jnp.sum(column * four, axis=0, keepdims=True)
        small[0, 8:16] = jnp.broadcast_to(line, (8, 128))
        ns = [start(small.at[0], scx.at[p], plane(*o)) for p, o in enumerate(others)]
        yield
        total = small[0]
        for p in range(7):
            arrived(ns[p], scx.at[p])
            total = total + scx[p]
        small[1] = total
        ns = [start(small.at[1], sz.at[i], owner_of(i)) for i in range(4)]
        yield
        for i in range(4):
            arrived(ns[i], sz.at[i])
        small[2] = (sz[0] + sz[1]) + (sz[2] + sz[3])
        for k, (axis, got) in enumerate((("y", sy), ("l", szl))):
            ns = [start(small.at[2 + k], got.at[d - 1], peer(axis, d)) for d in (1, 2, 3)]
            yield
            for d in (1, 2, 3):
                arrived(ns[d - 1], got.at[d - 1])
            small[3 + k] = (small[2 + k] + got[0]) + (got[1] + got[2])
        total = small[4] * POINT_SCALE
        spread = dot_exact(((iota((32, 8), 0) >> 2) == iota((32, 8), 1)).astype(F32), total[0:8])
        spread = jnp.where((iota((32, 128), 0) & 3) == (iota((32, 128), 1) >> 5), spread, 0.0)
        point_out[...] = dot_exact(spread, ((iota((128, 32), 0) & 31) == iota((128, 32), 1)).astype(F32))
        bias_out[...] = total[8:9, 0:32]

    def weight_sum():
        near = [lax.rem(zl + d, 4) for d in range(4)]
        ns = {
            d: [start(dw.at[lax.rem(yy + e, 4), near[d]], ry.at[e - 1, d], peer("y", e)) for e in (1, 2, 3)]
            for d in (2, 1, 3, 0)
        }
        yield
        zs = {}
        for d in (2, 1, 3, 0):
            for e in (1, 2, 3):
                arrived(ns[d][e - 1], ry.at[e - 1, d])
            dw1[d] = (dw[yy, near[d]] + ry[0, d]) + (ry[1, d] + ry[2, d])
            if d > 0:
                zs[d] = start(dw1.at[d], rzl.at[d - 1], peer("l", d))
        yield
        for d in (1, 2, 3):
            arrived(zs[d], rzl.at[d - 1])
        dwf[yy, zl] = ((dw1[0] + rzl[0]) + (rzl[1] + rzl[2])) * SAMPLE_SCALE
        here = dwf.at[yy, zl]
        zs = {d: start(here, here, peer("l", d)) for d in (2, 1, 3)}
        ns = {0: [start(here, here, peer("y", e)) for e in (1, 2, 3)]}
        yield
        for d in (1, 3, 2):
            here = dwf.at[yy, lax.rem(zl + 4 - d, 4)]
            arrived(zs[d], here)
            ns[d] = [start(here, here, peer("y", e)) for e in (1, 2, 3)]
        yield
        for d in (0, 1, 3, 2):
            for e in (1, 2, 3):
                arrived(ns[d][e - 1], dwf.at[lax.rem(yy + 4 - e, 4), lax.rem(zl + 4 - d, 4)])
        pltpu.make_async_copy(dwf, dw_out, local_sem.at[6]).start()

    a, b = chain_of(0), chain_of(1)
    smalls, weights = small_sum(), weight_sum()

    def go(*parts):
        for part in parts:
            next(part, None)

    go(a, b)
    loads[4].wait()
    loads[5].wait()
    point_tables()
    pl.semaphore_wait(barrier, len(greeted))
    go(a, b)
    later_tables()
    go(a, a, b, b)
    pointwise(0)
    pointwise(1)
    loads[3].wait()
    go(a, b)
    go(a, b)
    go(a, b)
    loads[2].wait()
    go(a)
    go(b)
    point_back(0)
    go(a, a, b, b)
    point_back(1)
    go(smalls)
    go(a, b)
    go(smalls)
    go(weights)
    go(a, b)
    go(a, b)
    go(weights)
    go(smalls)
    go(a)
    go(weights)
    go(smalls)
    go(b)
    go(smalls)
    go(weights)

    for copy in sends:
        copy.wait_send()
    pltpu.make_async_copy(ob.at[0], out_hbm.at[0], local_sem.at[4]).wait()
    pltpu.make_async_copy(ob.at[1], out_hbm.at[1], local_sem.at[5]).wait()
    pltpu.make_async_copy(dwf, dw_out, local_sem.at[6]).wait()


def place(grad, dw, point, bias, out, dw_out, point_out, bias_out, held, piece, whole, sem):
    loads = [pltpu.make_async_copy(grad.at[s], held.at[s], sem.at[s]) for s in range(2)]
    stores = [pltpu.make_async_copy(held.at[s], out.at[s], sem.at[2 + s]) for s in range(2)]
    load = pltpu.make_async_copy(dw, piece, sem.at[4])
    store = pltpu.make_async_copy(whole, dw_out, sem.at[5])
    load.start()
    for copy in loads:
        copy.start()
    point_out[...] = point[...]
    bias_out[...] = bias[...]
    load.wait()
    for b in range(2):
        for p in range(2):
            for q in range(4):
                whole[b, :, p, 256 * q:256 * q + 256] = piece[2 * b + p, q]
    store.start()
    for s in range(2):
        loads[s].wait()
        stores[s].start()
    for copy in [store] + stores:
        copy.wait()


COPIES = 4 * 36 + 17 + 30


def body(layer_input, cotangent, closure_step, spectral_weight, point_weight, bias):
    anywhere = pl.BlockSpec(memory_space=pl.ANY)
    vmem = pl.BlockSpec(memory_space=pltpu.VMEM)
    V = pltpu.VMEM
    scratch = [
        V((S, C, T, X), BF16), V((S, C, T, X), BF16), V((2, 16, 2, 1024), F32), V((C, C), F32), V((1, C), F32),
        V((S, C, T, X), F32), V((S, C, T, X), F32), V((S, C, T, X), BF16),
        V((256, 256), BF16), V((2, 2, 256, 256), BF16), V((2, 2, 256, 256), BF16), V((2, 512, 256), BF16),
        V((2, 256, 256), BF16), V((2, 256, 256), BF16),
        V((256, 512), BF16), V((512, 256), BF16), V((2, 256, 128), BF16), V((128, 512), BF16),
        V((256, 128), F32), V((256, 32), F32),
        V((S, 2, 8, 64, 256), BF16), V((S, 4, 256, 256), BF16), V((S, 2, 2, 2, 16, 512), F32),
        V((256, 256), F32), V((256, 128), F32),
        V((4, 2, 2, 4, 2, 8, 256), F32), V((4, 2, 7, 2, 8, 256), F32), V((4, 2, 2, 8, 256), F32),
        V((4, 4, 8, 256), F32), V((4, 8, 256), F32), V((4, 2, 2, 4, 2, 8, 256), F32),
        V((4, 4, 16, 256), F32), V((3, 4, 16, 256), F32), V((4, 16, 256), F32), V((3, 16, 256), F32),
        V((4, 4, 16, 256), F32),
        V((5, 16, 128), F32), V((7, 16, 128), F32), V((4, 16, 128), F32), V((3, 16, 128), F32), V((3, 16, 128), F32),
        pltpu.SemaphoreType.DMA((9,)), pltpu.SemaphoreType.DMA((COPIES,)), pltpu.SemaphoreType.DMA((COPIES,)),
    ]
    grad, dw, point, bias_grad = pl.pallas_call(
        kernel,
        out_shape=(
            jax.ShapeDtypeStruct((S, C, T, X), BF16),
            jax.ShapeDtypeStruct((4, 4, 16, 256), F32),
            jax.ShapeDtypeStruct((C, C), F32),
            jax.ShapeDtypeStruct((1, C), F32),
        ),
        in_specs=[anywhere, anywhere, pl.BlockSpec(memory_space=pltpu.SMEM), anywhere, anywhere, anywhere],
        out_specs=(anywhere, anywhere, vmem, vmem),
        scratch_shapes=scratch,
        compiler_params=pltpu.CompilerParams(
            collective_id=0, has_side_effects=True, vmem_limit_bytes=60 * 1024 * 1024
        ),
    )(layer_input, cotangent, closure_step, spectral_weight, point_weight, bias.reshape(1, C))
    grad, dw, point, bias_grad = pl.pallas_call(
        place,
        out_shape=(
            jax.ShapeDtypeStruct((S, C, T, X), BF16),
            jax.ShapeDtypeStruct((2, 16, 2, 1024), F32),
            jax.ShapeDtypeStruct((C, C), F32),
            jax.ShapeDtypeStruct((1, C), F32),
        ),
        in_specs=[anywhere, anywhere, vmem, vmem],
        out_specs=(anywhere, anywhere, vmem, vmem),
        scratch_shapes=[
            V((S, C, T, X), BF16), V((4, 4, 16, 256), F32), V((2, 16, 2, 1024), F32), pltpu.SemaphoreType.DMA((6,)),
        ],
        compiler_params=pltpu.CompilerParams(vmem_limit_bytes=60 * 1024 * 1024),
    )(grad, dw, point, bias_grad)
    return grad, dw, point, bias_grad.reshape(C)


def solution(mesh):
    return jax.shard_map(
        body,
        mesh=mesh,
        in_specs=(
            P("dp", None, None, "space"),
            P("dp", None, None, "space"),
            P("dp"),
            P("space", None, None, None),
            P(),
            P(),
        ),
        out_specs=(P("dp", None, None, "space"), P("space", None, None, None), P(), P()),
        check_vma=False,
    )
```

time: 103 us -> 87 us (0.84); the launches traced: 101 us -> 86.8 us
  local copies, waits for them, and re-layouts: 7.96 us -> 0 us
  Pallas kernels: 92.4 us -> 86.1 us
    pallas_call x1, Pallas kernels: 92.4 us -> 82.7 us  [body(): pl.pallas_call(kernel, out_shape=(jax.ShapeDtypeStruct((S, C, T, X), BF16...]
    unnamed x15 -> x0, local copies, waits for them, and re-layouts: 6.86 us -> none
    pallas_call x0 -> x1, Pallas kernels: none -> 3.47 us  [body(): pl.pallas_call(place, out_shape=(jax.ShapeDtypeStruct((S, C, T, X), BF16)...]
where the time goes in v2:
time: 87 us; the launch traced here: 86.8 us
  Pallas kernels  86.1 us (99%)
    pallas_call x1, Pallas kernels, body(): pl.pallas_call(kernel, out_shape=(jax.ShapeDtypeStruct((S, C, T, X), BF16...  82.7 us
    pallas_call x1, Pallas kernels, body(): pl.pallas_call(place, out_shape=(jax.ShapeDtypeStruct((S, C, T, X), BF16)...  3.47 us

profile of v2, /device:TPU:1, one launch (start us, length us, event | category | flops | bytes accessed | tf_op | source)
XLA Modules:
  0.0 86.8 jit_solution(2106266829998922594)
XLA Ops:
  0.6 82.7 %shard_map.93 = (bf16[2,32,64,128]{3,2,1,0:T(8,128)(2,1)}, f32[4,4,16,256]{3,2,1,0:T(8,128)}, f32[32,32]{1,0:T(8,128)}, f32[1,32]{1,0:T(1,128)}) custom-call(bf16[2,32,64,128]{3,2,1,0:T(8,128)(2,1)} %u_hbm.1, bf16[2,32,64,128]{3,2,1,0:T(8,128)(2,1)} %c_hbm.1, s32[2]{0:T(128)} %step_ref.1, f32[2,16,2,1024]{3,2,1,0:T(2,128)} %w_hbm.1, f32[32,32]{1,0:T(8,128)} %pw_ref.1, ...), custom_call_target="tpu_custom_call" | custom-call | tf_op jit(solution)/shard_map/pallas_call | solution.py:539
  83.3 3.5 %shard_map.94 = (bf16[2,32,64,128]{3,2,1,0:T(8,128)(2,1)}, f32[2,16,2,1024]{3,2,1,0:T(2,128)}, f32[32,32]{1,0:T(8,128)}, f32[1,32]{1,0:T(1,128)}) custom-call(bf16[2,32,64,128]{3,2,1,0:T(8,128)(2,1)} %get-tuple-element.12.grad, f32[4,4,16,256]{3,2,1,0:T(8,128)} %get-tuple-element.13.dw, f32[32,32]{1,0:T(8,128)} %get-tuple-element.14.point, ...), custom_call_target="tpu_custom_call" | custom-call | tf_op jit(solution)/shard_map/pallas_call | solution.py:554

commit v3 on v2

--- a/solution.py
+++ b/solution.py
@@ -448,29 +448,41 @@
         for part in parts:
             next(part, None)
 
-    go(a, b)
+    def sent(keep):
+        done = len(sends) - keep
+        for copy in sends[:done]:
+            copy.wait_send()
+        del sends[:done]
+
+    go(a)
+    pl.semaphore_wait(barrier, len(greeted))
+    go(a)
+    go(b)
+    go(b)
+    later_tables()
+    go(a, a, b, b)
     loads[4].wait()
     loads[5].wait()
     point_tables()
-    pl.semaphore_wait(barrier, len(greeted))
-    go(a, b)
-    later_tables()
-    go(a, a, b, b)
     pointwise(0)
     pointwise(1)
     loads[3].wait()
     go(a, b)
+    sent(16)
     go(a, b)
     go(a, b)
     loads[2].wait()
     go(a)
     go(b)
+    go(a, a)
     point_back(0)
-    go(a, a, b, b)
+    go(b, b)
     point_back(1)
     go(smalls)
+    sent(32)
     go(a, b)
     go(smalls)
+    sent(28)
     go(weights)
     go(a, b)
     go(a, b)
@@ -479,6 +491,7 @@
     go(a)
     go(weights)
     go(smalls)
+    sent(18)
     go(b)
     go(smalls)
     go(weights)

time: 87 us -> 85.5 us (0.983)
  Pallas kernels: 86.1 us -> 84.6 us
    pallas_call x1, Pallas kernels: 82.7 us -> 81.2 us  [body(): pl.pallas_call(kernel, out_shape=(jax.ShapeDtypeStruct((S, C, T, X), BF16...]
where the time goes in v3:
time: 85.5 us; the launch traced here: 85.3 us
  Pallas kernels  84.6 us (99%)
    pallas_call x1, Pallas kernels, body(): pl.pallas_call(kernel, out_shape=(jax.ShapeDtypeStruct((S, C, T, X), BF16...  81.2 us
    pallas_call x1, Pallas kernels, body(): pl.pallas_call(place, out_shape=(jax.ShapeDtypeStruct((S, C, T, X), BF16)...  3.47 us

profile of v3, /device:TPU:1, one launch (start us, length us, event | category | flops | bytes accessed | tf_op | source)
XLA Modules:
  0.0 85.3 jit_solution(10140377487615683296)
XLA Ops:
  0.6 81.2 %shard_map.93 = (bf16[2,32,64,128]{3,2,1,0:T(8,128)(2,1)}, f32[4,4,16,256]{3,2,1,0:T(8,128)}, f32[32,32]{1,0:T(8,128)}, f32[1,32]{1,0:T(1,128)}) custom-call(bf16[2,32,64,128]{3,2,1,0:T(8,128)(2,1)} %u_hbm.1, bf16[2,32,64,128]{3,2,1,0:T(8,128)(2,1)} %c_hbm.1, s32[2]{0:T(128)} %step_ref.1, f32[2,16,2,1024]{3,2,1,0:T(2,128)} %w_hbm.1, f32[32,32]{1,0:T(8,128)} %pw_ref.1, ...), custom_call_target="tpu_custom_call" | custom-call | tf_op jit(solution)/shard_map/pallas_call | solution.py:552
  81.8 3.5 %shard_map.94 = (bf16[2,32,64,128]{3,2,1,0:T(8,128)(2,1)}, f32[2,16,2,1024]{3,2,1,0:T(2,128)}, f32[32,32]{1,0:T(8,128)}, f32[1,32]{1,0:T(1,128)}) custom-call(bf16[2,32,64,128]{3,2,1,0:T(8,128)(2,1)} %get-tuple-element.12.grad, f32[4,4,16,256]{3,2,1,0:T(8,128)} %get-tuple-element.13.dw, f32[32,32]{1,0:T(8,128)} %get-tuple-element.14.point, ...), custom_call_target="tpu_custom_call" | custom-call | tf_op jit(solution)/shard_map/pallas_call | solution.py:567

commit v4 on v3

--- a/solution.py
+++ b/solution.py
@@ -175,7 +175,7 @@
             ab[s, 1, n, :, 128:256] = lo[64:]
             return carry
 
-        lax.fori_loop(0, 8, block, 0)
+        lax.fori_loop(0, 4, lambda n, carry: block(2 * n + 1, block(2 * n, carry)), 0)
         total = None
         for q in range(2):
             right = tuple(ab[s, p, 4 * q:4 * q + 4].reshape(256, 256) for p in range(2))
@@ -198,7 +198,7 @@
             finish(n, both[:, :128] + (both[:, 128:] + dot(d4[1], ul[s, n, 0:128], NT)))
             return carry
 
-        lax.fori_loop(0, 4, block, 0)
+        lax.fori_loop(0, 2, lambda n, carry: block(2 * n + 1, block(2 * n, carry)), 0)
 
     mask16 = ((iota((16, 256), 1) & 15) == iota((16, 256), 0)).astype(F32)
     mask512 = ((iota((16, 512), 1) & 15) == iota((16, 512), 0)).astype(F32)
@@ -493,8 +493,8 @@
     go(smalls)
     sent(18)
     go(b)
+    go(weights)
     go(smalls)
-    go(weights)
 
     for copy in sends:
         copy.wait_send()

time: 85.5 us -> 83 us (0.971)
  Pallas kernels: 84.6 us -> 82.2 us
    pallas_call x1, Pallas kernels: 81.2 us -> 78.7 us  [body(): pl.pallas_call(kernel, out_shape=(jax.ShapeDtypeStruct((S, C, T, X), BF16...]
where the time goes in v4:
time: 83 us; the launch traced here: 82.8 us
  Pallas kernels  82.2 us (99%)
    pallas_call x1, Pallas kernels, body(): pl.pallas_call(kernel, out_shape=(jax.ShapeDtypeStruct((S, C, T, X), BF16...  78.7 us
    pallas_call x1, Pallas kernels, body(): pl.pallas_call(place, out_shape=(jax.ShapeDtypeStruct((S, C, T, X), BF16)...  3.47 us

profile of v4, /device:TPU:1, one launch (start us, length us, event | category | flops | bytes accessed | tf_op | source)
XLA Modules:
  0.0 82.8 jit_solution(4425493779480129645)
XLA Ops:
  0.6 78.7 %shard_map.93 = (bf16[2,32,64,128]{3,2,1,0:T(8,128)(2,1)}, f32[4,4,16,256]{3,2,1,0:T(8,128)}, f32[32,32]{1,0:T(8,128)}, f32[1,32]{1,0:T(1,128)}) custom-call(bf16[2,32,64,128]{3,2,1,0:T(8,128)(2,1)} %u_hbm.1, bf16[2,32,64,128]{3,2,1,0:T(8,128)(2,1)} %c_hbm.1, s32[2]{0:T(128)} %step_ref.1, f32[2,16,2,1024]{3,2,1,0:T(2,128)} %w_hbm.1, f32[32,32]{1,0:T(8,128)} %pw_ref.1, ...), custom_call_target="tpu_custom_call" | custom-call | tf_op jit(solution)/shard_map/pallas_call | solution.py:552
  79.3 3.5 %shard_map.94 = (bf16[2,32,64,128]{3,2,1,0:T(8,128)(2,1)}, f32[2,16,2,1024]{3,2,1,0:T(2,128)}, f32[32,32]{1,0:T(8,128)}, f32[1,32]{1,0:T(1,128)}) custom-call(bf16[2,32,64,128]{3,2,1,0:T(8,128)(2,1)} %get-tuple-element.12.grad, f32[4,4,16,256]{3,2,1,0:T(8,128)} %get-tuple-element.13.dw, f32[32,32]{1,0:T(8,128)} %get-tuple-element.14.point, ...), custom_call_target="tpu_custom_call" | custom-call | tf_op jit(solution)/shard_map/pallas_call | solution.py:567
